TPU v7x, 1024 devices: a whole 4x8x16 slice. The times are simulated.
1024 devices in a mesh: dp: 32 (over y, x_hi, core), expert: 32 (over x_lo, z).
Axes of the slice: x: 4 (x_hi: 2, x_lo: 2; x = x_hi * 2 + x_lo), y: 8, z: 16, core: 2. Of those that a mesh axis runs over, the one named last changes fastest.
Arguments:
- cotangent: bfloat16 [131072, 3584], P(('dp', 'expert')), may hold values from -6 to 6
- gates: bfloat16 [131072, 1], P(('dp', 'expert')), may hold values from 0.049804688 to 1
- expert_ids: int32 [131072, 1], P(('dp', 'expert')), may hold values from 0 to 63; in each aligned block of 128 rows (0 to 127, 128 to 255, ...) at most 3 rows name the same one
- hidden: bfloat16 [32, 64, 32, 3, 2560], P('dp', 'expert'), may hold values from -6 to 6
- factor_a: bfloat16 [64, 2560, 128], P('expert'), may hold values from -0.125 to 0.125
- factor_b: bfloat16 [64, 128, 3584], P('expert'), may hold values from -0.5 to 0.5
Outputs:
- grad_a: float32 [64, 2560, 128], P('expert', 'dp')
- grad_b: float32 [64, 128, 3584], P('expert', None, 'dp')
- grad_hidden: bfloat16 [32, 64, 32, 3, 2560], P('dp', 'expert')
- grad_gates: float32 [131072, 1], P(('dp', 'expert'))
Inputs may be any that keep to these rules, and one draw needn't show every extreme that they name: `expert_ids`: among the 128 tokens of one device no expert is named more than 3 times, a bound that some block reaches.
All inputs are finite; a program needn't handle non-finite values.
Results may differ from a plain program's by a relative error of at most 0.0057.
Values may be sent and summed in bfloat16 or wider, within the bound.
No kernel may reach another device: no remote copies, remote signals or barrier semaphores. Data moves between devices by JAX's collectives and lax.ppermute only.
A program may use at most 64 MiB of HBM per device.

v0:
```python
import jax
import jax.numpy as jnp
from jax import lax
from jax.experimental import pallas as pl
from jax.experimental.pallas import tpu as pltpu
from jax.sharding import Mesh, PartitionSpec as P

CAP = 3
ROWS = 4
RIDE = 16
VMEM = 60 * 2**20
EXPERT = ("x", "z")
SIDES = ("k",) + EXPERT
GROUPS = ("q", "k")


def place_kernel(ids_ref, gate_ref, dy_hbm, send_hbm, row_ref, dy, send, in_sem, out_sem):
    experts = send_hbm.shape[0]
    tokens, width = dy.shape
    quarter = width // ROWS

    def fetch(c):
        part = (slice(None), pl.ds(c * quarter, quarter))
        return pltpu.make_async_copy(dy_hbm.at[part], dy.at[part], in_sem.at[c])

    def store(c):
        part = (slice(None), slice(None), pl.ds(c * quarter, quarter))
        return pltpu.make_async_copy(send.at[part], send_hbm.at[part], out_sem.at[c])

    for c in (CAP, *range(CAP)):
        fetch(c).start()
    ids = ids_ref[...]
    expert = lax.broadcasted_iota(jnp.int32, (experts, tokens), 0)
    named = expert == ids
    older = lax.broadcasted_iota(jnp.int32, (tokens, tokens), 0)
    newer = lax.broadcasted_iota(jnp.int32, (tokens, tokens), 1)
    before = jnp.dot(
        named.astype(jnp.bfloat16),
        (older < newer).astype(jnp.bfloat16),
        preferred_element_type=jnp.float32,
    )
    rank = jnp.sum(jnp.where(named, before, 0.0), axis=0, keepdims=True).astype(jnp.int32)
    row_ref[...] = rank
    block = (ids % 2) * (experts // 2) + ids // 2
    row = lax.broadcasted_iota(jnp.int32, (experts * ROWS, tokens), 0)
    whole = row == block * ROWS + rank
    last = row == block * ROWS + CAP
    gates = jnp.broadcast_to(gate_ref[...].astype(jnp.float32), whole.shape)
    fetch(CAP).wait()
    for c in range(CAP):
        rest = last & (rank == c)
        gate = jnp.sum(jnp.where(whole | rest, gates, 0.0), axis=1, keepdims=True)
        pick = jnp.concatenate([whole.astype(jnp.bfloat16), rest.astype(jnp.bfloat16)], axis=1)
        fetch(c).wait()
        columns = slice(c * quarter, (c + 1) * quarter)
        rows = jnp.dot(
            pick,
            jnp.concatenate([dy[:, columns], dy[:, CAP * quarter :]], axis=0),
            preferred_element_type=jnp.float32,
        )
        send[:, :, columns] = (rows * gate).astype(jnp.bfloat16).reshape(experts, ROWS, quarter)
        store(c).start()
    for c in range(CAP):
        store(c).wait()


def place(ids, gates, cotangent, experts):
    tokens, width = cotangent.shape
    shape = (experts, ROWS, CAP * (width // ROWS))
    whole = pl.BlockSpec(memory_space=pltpu.VMEM)
    return pl.pallas_call(
        place_kernel,
        in_specs=[whole, whole, pl.BlockSpec(memory_space=pl.ANY)],
        out_specs=[pl.BlockSpec(memory_space=pl.ANY), whole],
        out_shape=[
            jax.ShapeDtypeStruct(shape, jnp.bfloat16),
            jax.ShapeDtypeStruct((1, tokens), jnp.int32),
        ],
        scratch_shapes=[
            pltpu.VMEM((tokens, width), jnp.bfloat16),
            pltpu.VMEM(shape, jnp.bfloat16),
            pltpu.SemaphoreType.DMA((ROWS,)),
            pltpu.SemaphoreType.DMA((CAP,)),
        ],
        compiler_params=pltpu.CompilerParams(vmem_limit_bytes=VMEM),
        name="place_rows",
    )(ids, gates, cotangent)


def grads_kernel(
    core_ref, got_hbm, b_ref, low_ref, rest_ref, back_ref, hidden, out, gl_ref, got, got_sem
):
    slots, rank = low_ref.shape
    core, width = core_ref[0], b_ref.shape[2]
    quarter = width // ROWS
    across = (((1,), (1,)), ((), ()))
    down = (((0,), (0,)), ((), ()))
    cut = out.shape[0]
    a_rows = hidden.shape[1] // cut
    b_rows = width // cut
    per = cut // ROWS

    def fetch(c):
        columns = pl.ds(c * quarter, quarter)
        return pltpu.make_async_copy(
            got_hbm.at[:, :, columns], got.at[:, :, columns], got_sem.at[c]
        )

    for c in range(CAP):
        fetch(c).start()
    place_in = lax.broadcasted_iota(jnp.int32, (slots, rank), 0) % ROWS
    low = low_ref[...]
    total = jnp.zeros((slots, rank), jnp.float32)
    last = jnp.zeros((quarter, rank), jnp.float32)
    for c in range(CAP):
        fetch(c).wait()
        x = got[:, :, c * quarter : (c + 1) * quarter].reshape(slots, quarter)
        main = lax.dot_general(
            x,
            b_ref[core, :, c * quarter : (c + 1) * quarter],
            across,
            preferred_element_type=jnp.float32,
        )
        rest = lax.dot_general(
            x, b_ref[core, :, CAP * quarter :], across, preferred_element_type=jnp.float32
        )
        total = total + jnp.where(place_in < CAP, main, 0.0)
        rest = jnp.concatenate([rest[CAP - c :], rest[: CAP - c]], axis=0)
        total = total + jnp.where(place_in == c, rest, 0.0)
        both = lax.dot_general(
            x,
            jnp.concatenate([low, rest_ref[c]], axis=1),
            down,
            preferred_element_type=jnp.float32,
        )
        last = last + both[:, rank:]
        out[c * per : (c + 1) * per, a_rows:, :] = (
            both[:, :rank].astype(jnp.bfloat16).reshape(per, b_rows, rank)
        )
    out[CAP * per :, a_rows:, :] = last.astype(jnp.bfloat16).reshape(per, b_rows, rank)

    grad_low = jnp.dot(
        back_ref[...], total.astype(jnp.bfloat16), preferred_element_type=jnp.float32
    ).astype(jnp.bfloat16)
    out[:, :a_rows, :] = (
        lax.dot_general(hidden[...], grad_low, down, preferred_element_type=jnp.float32)
        .astype(jnp.bfloat16)
        .reshape(cut, a_rows, rank)
    )
    sg = lax.dot_general(
        jnp.ones((RIDE, rank), jnp.float32),
        total * low.astype(jnp.float32),
        across,
        precision=lax.Precision.HIGHEST,
        preferred_element_type=jnp.float32,
    )
    head = sg.astype(jnp.bfloat16).astype(jnp.float32)
    line = lax.broadcasted_iota(jnp.int32, sg.shape, 0)
    ride = jnp.where(line == 0, head, jnp.where(line == 1, sg - head, 0.0)).astype(jnp.bfloat16)
    count = grad_low.shape[0] // 2
    for group in range(2):
        gl_ref[group, :count] = grad_low[group * count : (group + 1) * count]
        gl_ref[group, count:] = ride[:, group * (slots // 2) : (group + 1) * (slots // 2)]


def slot_grads(core, got, b, low, rest, back, hidden, cut):
    slots, rank = low.shape
    rows = (hidden.shape[1] + b.shape[2]) // cut
    whole = pl.BlockSpec(memory_space=pltpu.VMEM)
    return pl.pallas_call(
        grads_kernel,
        in_specs=[pl.BlockSpec(memory_space=pltpu.SMEM), pl.BlockSpec(memory_space=pl.ANY)]
        + [whole] * 5,
        out_specs=[whole, whole],
        out_shape=[
            jax.ShapeDtypeStruct((cut, rows, rank), jnp.bfloat16),
            jax.ShapeDtypeStruct((2, hidden.shape[0] // 2 + RIDE, rank), jnp.bfloat16),
        ],
        scratch_shapes=[
            pltpu.VMEM(got.shape, jnp.bfloat16),
            pltpu.SemaphoreType.DMA((CAP,)),
        ],
        compiler_params=pltpu.CompilerParams(vmem_limit_bytes=48 * 2**20),
        name="slot_grads",
    )(core.reshape(1), got, b, low, rest, back, hidden)


def add_kernel(parts_ref, a_ref, b_ref):
    total = jnp.sum(parts_ref[...].astype(jnp.float32), axis=0)
    a_rows = a_ref.shape[1]
    a_ref[...] = total[:, :a_rows]
    b_ref[...] = total[:, a_rows:]


def add_parts(parts, a_rows):
    count, rows, rank = parts.shape
    b_rows = rows - a_rows
    return pl.pallas_call(
        add_kernel,
        grid=(2,),
        in_specs=[pl.BlockSpec((count // 2, 1, rows, rank), lambda i: (0, i, 0, 0))],
        out_specs=[
            pl.BlockSpec((1, a_rows, rank), lambda i: (i, 0, 0)),
            pl.BlockSpec((1, b_rows, rank), lambda i: (i, 0, 0)),
        ],
        out_shape=[
            jax.ShapeDtypeStruct((2, a_rows, rank), jnp.float32),
            jax.ShapeDtypeStruct((2, b_rows, rank), jnp.float32),
        ],
        compiler_params=pltpu.CompilerParams(vmem_limit_bytes=63 * 2**20),
        name="add_parts",
    )(parts.reshape(count // 2, 2, rows, rank))


def body(cotangent, gates, expert_ids, hidden, factor_a, factor_b):
    tokens = cotangent.shape[0]
    sources = lax.axis_size("x") * lax.axis_size("z")
    experts = 2 * sources
    groups = 2 * lax.axis_size("q")
    core = lax.axis_index("k")
    units, rank = factor_a.shape[1], factor_a.shape[2]
    width = factor_b.shape[2]
    a_rows = units // groups
    pair = [(0, 1), (1, 0)]

    send, row = place(expert_ids.reshape(1, tokens), gates.reshape(1, tokens), cotangent, experts)
    got = lax.all_to_all(send, SIDES, split_axis=0, concat_axis=0, tiled=True)

    saved = jnp.transpose(hidden[0], (0, 2, 1, 3)).reshape(2, CAP * sources, units)
    own = lax.dynamic_index_in_dim(saved, core, 0, keepdims=False)
    other = lax.ppermute(
        lax.dynamic_index_in_dim(saved, 1 - core, 0, keepdims=False), "k", pair
    )
    mine = jnp.where(core == 0, jnp.stack([own, other]), jnp.stack([other, own]))
    a_mine = lax.dynamic_index_in_dim(factor_a, core, 0, keepdims=False)
    low = jnp.einsum("gsf,fr->gsr", mine, a_mine, preferred_element_type=jnp.float32).astype(
        jnp.bfloat16
    )
    low = low.reshape(2, CAP, sources, rank)
    by_source = jnp.transpose(low, (0, 2, 1, 3)).reshape(experts, CAP, rank)
    whole = jnp.pad(by_source, ((0, 0), (0, 1), (0, 0))).reshape(experts * ROWS, rank)
    rest = jnp.pad(
        jnp.transpose(by_source, (1, 0, 2))[:, :, None, :], ((0, 0), (0, 0), (CAP, 0), (0, 0))
    ).reshape(CAP, experts * ROWS, rank)
    slot = jnp.arange(experts * CAP, dtype=jnp.int32)
    group, place_c, source = slot // (CAP * sources), slot // sources % CAP, slot % sources
    at_row = (group * sources + source) * ROWS + place_c
    back_rows = (
        at_row[:, None] == jnp.arange(experts * ROWS, dtype=jnp.int32)[None, :]
    ).astype(jnp.bfloat16)

    parts, grad_low = slot_grads(
        core, got, factor_b, whole, rest, back_rows, mine.reshape(2 * CAP * sources, units), groups
    )
    summed = lax.all_to_all(parts, GROUPS, split_axis=0, concat_axis=0, tiled=True)
    grad_a, grad_b = add_parts(summed, a_rows)
    grad_b = jnp.transpose(grad_b, (0, 2, 1))

    kept = lax.dynamic_index_in_dim(grad_low, core, 0, keepdims=False)
    sent = lax.ppermute(
        lax.dynamic_index_in_dim(grad_low, 1 - core, 0, keepdims=False), "k", pair
    )
    count = CAP * sources
    line, side = lax.axis_size("z"), lax.axis_index("x")
    riding = jnp.concatenate([kept[count : count + 2], sent[count : count + 2]])
    along = lax.all_gather(riding, "z", axis=0, tiled=True)
    along = jnp.sum(along.reshape(2 * line, 2, 2 * line * ROWS).astype(jnp.float32), axis=1)
    target = (jnp.arange(2, dtype=jnp.int32) ^ side) * line + lax.axis_index("z")
    columns = target[:, None] * ROWS + jnp.arange(ROWS, dtype=jnp.int32)[None, :]
    pick = (
        jnp.arange(2 * line * ROWS, dtype=jnp.int32)[:, None, None] == columns[None]
    ).astype(jnp.float32)
    home = jnp.einsum("zs,sdr->dzr", along, pick, precision=lax.Precision.HIGHEST)
    home = jnp.stack([home[0], lax.ppermute(home[1], "x", pair)])
    ids = expert_ids.reshape(tokens)
    owner = ids // 2
    entry = ((owner // line) ^ side) * line + owner % line
    entry = (entry * 2 + ((ids % 2) ^ core)) * ROWS + row.reshape(tokens)
    chosen = (
        entry[:, None] == jnp.arange(experts * ROWS, dtype=jnp.int32)[None, :]
    ).astype(jnp.float32)
    grad_gates = jnp.dot(
        chosen, home.reshape(experts * ROWS, 1), precision=lax.Precision.HIGHEST
    ) / gates.astype(jnp.float32)

    kept, sent = kept[:count], sent[:count]
    grad_low = jnp.where(core == 0, jnp.stack([kept, sent]), jnp.stack([sent, kept]))
    grad_hidden = jnp.einsum(
        "lsr,lfr->lsf", grad_low, factor_a, preferred_element_type=jnp.float32
    ).astype(jnp.bfloat16)
    grad_hidden = jnp.transpose(grad_hidden.reshape(2, CAP, sources, units), (0, 2, 1, 3))
    return grad_a, grad_b, grad_hidden[None], grad_gates


def solution(mesh):
    groups, sources = mesh.shape["dp"], mesh.shape["expert"]
    fine = Mesh(
        mesh.devices.reshape(groups // 2, 2, 2, sources // 2), ("q", "k", "x", "z")
    )
    dp = GROUPS
    tokens = P(("q", "k", "x", "z"), None)
    return jax.shard_map(
        body,
        mesh=fine,
        in_specs=(
            tokens,
            tokens,
            tokens,
            P(dp, EXPERT, None, None, None),
            P(EXPERT, None, None),
            P(EXPERT, None, None),
        ),
        out_specs=(
            P(EXPERT, dp, None),
            P(EXPERT, None, dp),
            P(dp, EXPERT, None, None, None),
            tokens,
        ),
        check_vma=False,
    )
```

profile of v0, /device:TPU:1, one launch (start us, length us, event | category | flops | bytes accessed | tf_op | source)
XLA Modules:
  0.0 151.8 jit_solution(7547333586144298256)
XLA Ops:
  0.6 4.0 %place_rows.1 = (bf16[64,4,2688]{2,1,0:T(4,128)(2,1)}, s32[1,128]{1,0:T(1,128)}) custom-call(s32[1,128]{1,0:T(1,128)} %bitcast.75, bf16[1,128]{1,0:T(2,128)(2,1)} %bitcast.77, bf16[128,3584]{1,0:T(8,128)(2,1)} %dy_hbm.1), custom_call_target="tpu_custom_call" | custom-call | tf_op jit(solution)/shard_map/place_rows/pallas_call | solution.py:71
  4.7 0.0 copy-start.3
  4.7 22.0 %all-to-all-start = ((bf16[64,4,2688]{2,1,0:T(4,128)(2,1)}), bf16[64,4,2688]{2,1,0:T(4,128)(2,1)S(1)}, u32[]{:S(2)}, u32[]{:S(2)}) async-start(bf16[64,4,2688]{2,1,0:T(4,128)(2,1)} %get-tuple-element.10), calls=%async_computation | async-start | bytes 2752512 | tf_op jit(solution)/shard_map/all_to_all | solution.py:227
  26.7 0.0 copy-done.3
  26.7 0.8 constant_dynamic-slice_fusion.2
  27.6 2.3 %collective-permute-start = (bf16[96,2560]{1,0:T(8,128)(2,1)}, bf16[96,2560]{1,0:T(8,128)(2,1)S(1)}, u32[]{:S(2)}, u32[]{:S(2)}) collective-permute-start(bf16[96,2560]{1,0:T(8,128)(2,1)} %get-tuple-element.17), channel_id=1, source_target_pairs={{0,32},{32,0},{1,33},{33,1},{2,34},{34,2},{3,35},{35,3},{4,36},{36... | collective-permute-start | bytes 1474568 | tf_op jit(solution)/shard_map/ppermute | solution.py:231
  29.8 0.1 fusion.3.back_ref
  29.9 1.6 %collective-permute-done = bf16[96,2560]{1,0:T(8,128)(2,1)S(1)} collective-permute-done((bf16[96,2560]{1,0:T(8,128)(2,1)}, bf16[96,2560]{1,0:T(8,128)(2,1)S(1)}, u32[]{:S(2)}, u32[]{:S(2)}) %collective-permute-start) | collective-permute-done | bytes 491552 | tf_op jit(solution)/shard_map/ppermute | solution.py:231
  31.5 0.2 maximum_select_fusion
  31.7 1.5 convolution_convert_fusion.1
  33.2 0.1 copy.21
  33.3 0.1 pad.9.clone
  33.5 60.2 %all-to-all-done.got_hbm = bf16[64,4,2688]{2,1,0:T(4,128)(2,1)S(1)} async-done(((bf16[64,4,2688]{2,1,0:T(4,128)(2,1)}), bf16[64,4,2688]{2,1,0:T(4,128)(2,1)S(1)}, u32[]{:S(2)}, u32[]{:S(2)}) %all-to-all-start) | async-done | bytes 1376288 | tf_op jit(solution)/shard_map/all_to_all | solution.py:227
  93.7 0.0 copy-start
  93.7 1.5 copy-done
  95.2 2.8 %slot_grads.1 = (bf16[32,192,128]{2,1,0:T(8,128)(2,1)S(1)}, bf16[2,112,128]{2,1,0:T(8,128)(2,1)S(1)}) custom-call(s32[1]{0:T(128)} %bitcast.core_ref, bf16[64,4,2688]{2,1,0:T(4,128)(2,1)S(1)} %all-to-all-done.got_hbm, bf16[2,128,3584]{2,1,0:T(8,128)(2,1)S(1)} %copy-done, bf16[256,128]{1,0:T(8,128)(2,1)S(1)} %bitcast.67, bf16[3,256,128]{2,1,0:T(8,128)(2,1)S(1)} %bitcast.66, ...), custom_call_target="tpu_custom_call" | custom-call | tf_op jit(solution)/shard_map/slot_grads/pallas_call | solution.py:170
  98.0 0.0 copy-start.1
  98.0 1.1 copy-done.1
  99.2 0.0 copy-start.4
  99.2 0.0 copy-start.6
  99.2 0.0 copy-start.2
  99.2 11.3 %all-to-all-start.1 = ((bf16[32,192,128]{2,1,0:T(8,128)(2,1)}), bf16[32,192,128]{2,1,0:T(8,128)(2,1)}, u32[]{:S(2)}, u32[]{:S(2)}) async-start(bf16[32,192,128]{2,1,0:T(8,128)(2,1)} %copy-done.1), calls=%async_computation.1 | async-start | bytes 3145728 | tf_op jit(solution)/shard_map/all_to_all | solution.py:255
  110.4 0.0 copy-start.5
  110.5 0.1 iota_add_fusion
  110.5 0.0 copy-done.4
  110.5 0.0 copy-done.6
  110.6 2.2 %collective-permute-start.1 = (bf16[112,128]{1,0:T(8,128)(2,1)S(1)}, bf16[112,128]{1,0:T(8,128)(2,1)S(1)}, u32[]{:S(2)}, u32[]{:S(2)}) collective-permute-start(bf16[112,128]{1,0:T(8,128)(2,1)S(1)} %dynamic-slice_bitcast_fusion.1), channel_id=1, source_target_pairs={{0,32},{32,0},{1,33},{33,1},{2,34},{34,2},{3,35},{35,3},{4,36},{36... | collective-permute-start | bytes 86024 | tf_op jit(solution)/shard_map/ppermute | solution.py:260
  112.8 0.8 collective-permute-done.1
  113.7 23.1 %all-gather = bf16[16,4,128]{2,1,0:T(4,128)(2,1)S(1)} all-gather(bf16[1,4,128]{2,1,0:T(4,128)(2,1)S(1)} %maximum_bitcast_fusion), channel_id=1, replica_groups=mesh['q'=16,'k'=2,'x'=2,'z'=16] {'z'}, dimensions={0}, use_global_device_ids=true | all-gather | bytes 17408 | tf_op jit(solution)/shard_map/all_gather | solution.py:266
  136.9 0.2 convolution_bitcast_fusion
  137.1 2.8 %collective-permute-start.2 = (f32[32,4]{0,1:T(4,128)S(1)}, f32[32,4]{0,1:T(4,128)S(1)}, u32[]{:S(2)}, u32[]{:S(2)}) collective-permute-start(f32[32,4]{0,1:T(4,128)S(1)} %get-tuple-element.19), channel_id=1, source_target_pairs={{0,16},{16,0},{1,17},{17,1},{2,18},{18,2},{3,19},{19,3},{4,20},{20... | collective-permute-start | bytes 1544 | tf_op jit(solution)/shard_map/ppermute | solution.py:274
  139.9 0.0 copy-done.2
  139.9 1.5 convolution_convert_fusion
  141.4 0.4 collective-permute-done.2
  141.8 0.1 copy.19
  141.9 0.1 reshape.144
  142.0 0.0 copy-done.5
  142.0 0.8 fusion
  142.8 6.9 %all-to-all-done.1 = bf16[32,192,128]{2,1,0:T(8,128)(2,1)} async-done(((bf16[32,192,128]{2,1,0:T(8,128)(2,1)}), bf16[32,192,128]{2,1,0:T(8,128)(2,1)}, u32[]{:S(2)}, u32[]{:S(2)}) %all-to-all-start.1) | async-done | bytes 1572896 | tf_op jit(solution)/shard_map/all_to_all | solution.py:255
  149.7 2.1 %add_parts.1 = (f32[2,80,128]{2,1,0:T(8,128)}, f32[2,112,128]{2,1,0:T(8,128)}) custom-call(bf16[16,2,192,128]{3,2,1,0:T(8,128)(2,1)} %bitcast.20.parts_ref), custom_call_target="tpu_custom_call" | custom-call | tf_op jit(solution)/shard_map/add_parts/pallas_call | solution.py:198
  (15 shorter events, 0.2 us)
Async XLA Ops:
  4.7 22.0 %copy-start.3 = (bf16[1,2,32,3,2560]{4,2,3,1,0:T(8,128)(2,1)S(1)}, bf16[1,2,32,3,2560]{4,2,3,1,0:T(8,128)(2,1)}, u32[]{:S(2)}) copy-start(bf16[1,2,32,3,2560]{4,2,3,1,0:T(8,128)(2,1)} %param.9) | copy-start | bytes 2949124
  4.7 89.0 %all-to-all-start = ((bf16[64,4,2688]{2,1,0:T(4,128)(2,1)}), bf16[64,4,2688]{2,1,0:T(4,128)(2,1)S(1)}, u32[]{:S(2)}, u32[]{:S(2)}) async-start(bf16[64,4,2688]{2,1,0:T(4,128)(2,1)} %get-tuple-element.10), calls=%async_computation | async-start | bytes 2752512 | tf_op jit(solution)/shard_map/all_to_all | solution.py:227
  27.6 4.0 %collective-permute-start = (bf16[96,2560]{1,0:T(8,128)(2,1)}, bf16[96,2560]{1,0:T(8,128)(2,1)S(1)}, u32[]{:S(2)}, u32[]{:S(2)}) collective-permute-start(bf16[96,2560]{1,0:T(8,128)(2,1)} %get-tuple-element.17), channel_id=1, source_target_pairs={{0,32},{32,0},{1,33},{33,1},{2,34},{34,2},{3,35},{35,3},{4,36},{36... | collective-permute-start | bytes 1474568 | tf_op jit(solution)/shard_map/ppermute | solution.py:231
  93.7 1.5 copy-start
  98.0 1.1 copy-start.1
  99.2 11.4 %copy-start.4 = (s32[128,1]{0,1:T(1,128)S(1)}, s32[128,1]{0,1:T(1,128)}, u32[]{:S(2)}) copy-start(s32[128,1]{0,1:T(1,128)} %param.8) | copy-start | bytes 1540
  99.2 11.4 %copy-start.6 = (s32[1,128]{1,0:T(1,128)S(1)}, s32[1,128]{1,0:T(1,128)}, u32[]{:S(2)}) copy-start(s32[1,128]{1,0:T(1,128)} %get-tuple-element.15) | copy-start | bytes 1540
  99.2 40.7 %copy-start.2 = (bf16[2,2560,128]{2,1,0:T(8,128)(2,1)S(1)}, bf16[2,2560,128]{2,1,0:T(8,128)(2,1)}, u32[]{:S(2)}) copy-start(bf16[2,2560,128]{2,1,0:T(8,128)(2,1)} %param.10) | copy-start | bytes 3932164
  99.2 50.5 %all-to-all-start.1 = ((bf16[32,192,128]{2,1,0:T(8,128)(2,1)}), bf16[32,192,128]{2,1,0:T(8,128)(2,1)}, u32[]{:S(2)}, u32[]{:S(2)}) async-start(bf16[32,192,128]{2,1,0:T(8,128)(2,1)} %copy-done.1), calls=%async_computation.1 | async-start | bytes 3145728 | tf_op jit(solution)/shard_map/all_to_all | solution.py:255
  110.4 31.6 %copy-start.5 = (bf16[128,1]{0,1:T(2,128)(2,1)S(1)}, bf16[128,1]{0,1:T(2,128)(2,1)}, u32[]{:S(2)}) copy-start(bf16[128,1]{0,1:T(2,128)(2,1)} %param.7) | copy-start | bytes 772
  110.6 3.1 %collective-permute-start.1 = (bf16[112,128]{1,0:T(8,128)(2,1)S(1)}, bf16[112,128]{1,0:T(8,128)(2,1)S(1)}, u32[]{:S(2)}, u32[]{:S(2)}) collective-permute-start(bf16[112,128]{1,0:T(8,128)(2,1)S(1)} %dynamic-slice_bitcast_fusion.1), channel_id=1, source_target_pairs={{0,32},{32,0},{1,33},{33,1},{2,34},{34,2},{3,35},{35,3},{4,36},{36... | collective-permute-start | bytes 86024 | tf_op jit(solution)/shard_map/ppermute | solution.py:260
  137.1 4.7 %collective-permute-start.2 = (f32[32,4]{0,1:T(4,128)S(1)}, f32[32,4]{0,1:T(4,128)S(1)}, u32[]{:S(2)}, u32[]{:S(2)}) collective-permute-start(f32[32,4]{0,1:T(4,128)S(1)} %get-tuple-element.19), channel_id=1, source_target_pairs={{0,16},{16,0},{1,17},{17,1},{2,18},{18,2},{3,19},{19,3},{4,20},{20... | collective-permute-start | bytes 1544 | tf_op jit(solution)/shard_map/ppermute | solution.py:274
where the time goes:
time: 152 us
  waiting for transfers between devices  69.9 us (46%)
  starting transfers between devices  40.5 us (27%)
  blocking collectives  23.1 us (15%)
  Pallas kernels  8.95 us (6%)
  local copies, waits for them, and re-layouts  4.05 us (3%)
  matrix products  3.97 us (3%)
    all_to_all x1, waiting for transfers between devices, body(): got = lax.all_to_all(send, SIDES, split_axis=0, concat_axis=0, tiled=True)  60.2 us
    all_gather x1, blocking collectives, body(): along = lax.all_gather(riding, 'z', axis=0, tiled=True)  23.1 us
    all_to_all x1, starting transfers between devices, body(): got = lax.all_to_all(send, SIDES, split_axis=0, concat_axis=0, tiled=True)  22 us
    all_to_all x1, starting transfers between devices, body(): lax.all_to_all(parts, GROUPS, split_axis=0, concat_axis=0, tiled=True)  11.3 us
    all_to_all x1, waiting for transfers between devices, body(): lax.all_to_all(parts, GROUPS, split_axis=0, concat_axis=0, tiled=True)  6.88 us
    pallas_call x1, Pallas kernels, place(): pl.pallas_call(place_kernel, in_specs=[whole, whole, pl.BlockSpec(memory_...  4.04 us
  transfers between devices with their start and end apart: 5, of which 5 were waited for; matrix products, arithmetic and copies ran while one was open for 4% of the time, Pallas kernels for 0%

commit v1 on v0

--- a/solution.py
+++ b/solution.py
@@ -8,7 +8,6 @@
 CAP = 3
 ROWS = 4
 RIDE = 16
-VMEM = 60 * 2**20
 EXPERT = ("x", "z")
 SIDES = ("k",) + EXPERT
 GROUPS = ("q", "k")
@@ -82,7 +81,6 @@
             pltpu.SemaphoreType.DMA((ROWS,)),
             pltpu.SemaphoreType.DMA((CAP,)),
         ],
-        compiler_params=pltpu.CompilerParams(vmem_limit_bytes=VMEM),
         name="place_rows",
     )(ids, gates, cotangent)
 
@@ -180,7 +178,7 @@
             pltpu.VMEM(got.shape, jnp.bfloat16),
             pltpu.SemaphoreType.DMA((CAP,)),
         ],
-        compiler_params=pltpu.CompilerParams(vmem_limit_bytes=48 * 2**20),
+        compiler_params=pltpu.CompilerParams(vmem_limit_bytes=24 * 2**20),
         name="slot_grads",
     )(core.reshape(1), got, b, low, rest, back, hidden)
 

time: 152 us -> 152 us (level)
  no operation moved by 1% of the time
where the time goes in v1:
time: 152 us
  waiting for transfers between devices  69.9 us (46%)
  starting transfers between devices  40.5 us (27%)
  blocking collectives  23.1 us (15%)
  Pallas kernels  8.95 us (6%)
  local copies, waits for them, and re-layouts  4.05 us (3%)
  matrix products  3.97 us (3%)
    all_to_all x1, waiting for transfers between devices, body(): got = lax.all_to_all(send, SIDES, split_axis=0, concat_axis=0, tiled=True)  60.2 us
    all_gather x1, blocking collectives, body(): along = lax.all_gather(riding, 'z', axis=0, tiled=True)  23.1 us
    all_to_all x1, starting transfers between devices, body(): got = lax.all_to_all(send, SIDES, split_axis=0, concat_axis=0, tiled=True)  22 us
    all_to_all x1, starting transfers between devices, body(): lax.all_to_all(parts, GROUPS, split_axis=0, concat_axis=0, tiled=True)  11.3 us
    all_to_all x1, waiting for transfers between devices, body(): lax.all_to_all(parts, GROUPS, split_axis=0, concat_axis=0, tiled=True)  6.88 us
    pallas_call x1, Pallas kernels, place(): pl.pallas_call(place_kernel, in_specs=[whole, whole, pl.BlockSpec(memory_...  4.04 us
  transfers between devices with their start and end apart: 5, of which 5 were waited for; matrix products, arithmetic and copies ran while one was open for 4% of the time, Pallas kernels for 0%

profile of v1, /device:TPU:1, one launch (start us, length us, event | category | flops | bytes accessed | tf_op | source)
XLA Modules:
  0.0 151.8 jit_solution(3245498346803237521)
XLA Ops:
  0.6 4.0 %place_rows.1 = (bf16[64,4,2688]{2,1,0:T(4,128)(2,1)}, s32[1,128]{1,0:T(1,128)}) custom-call(s32[1,128]{1,0:T(1,128)} %bitcast.75, bf16[1,128]{1,0:T(2,128)(2,1)} %bitcast.77, bf16[128,3584]{1,0:T(8,128)(2,1)} %dy_hbm.1), custom_call_target="tpu_custom_call" | custom-call | tf_op jit(solution)/shard_map/place_rows/pallas_call | solution.py:70
  4.7 0.0 copy-start.3
  4.7 22.0 %all-to-all-start = ((bf16[64,4,2688]{2,1,0:T(4,128)(2,1)}), bf16[64,4,2688]{2,1,0:T(4,128)(2,1)S(1)}, u32[]{:S(2)}, u32[]{:S(2)}) async-start(bf16[64,4,2688]{2,1,0:T(4,128)(2,1)} %get-tuple-element.10), calls=%async_computation | async-start | bytes 2752512 | tf_op jit(solution)/shard_map/all_to_all | solution.py:225
  26.7 0.0 copy-done.3
  26.7 0.8 constant_dynamic-slice_fusion.2
  27.6 2.3 %collective-permute-start = (bf16[96,2560]{1,0:T(8,128)(2,1)}, bf16[96,2560]{1,0:T(8,128)(2,1)S(1)}, u32[]{:S(2)}, u32[]{:S(2)}) collective-permute-start(bf16[96,2560]{1,0:T(8,128)(2,1)} %get-tuple-element.17), channel_id=1, source_target_pairs={{0,32},{32,0},{1,33},{33,1},{2,34},{34,2},{3,35},{35,3},{4,36},{36... | collective-permute-start | bytes 1474568 | tf_op jit(solution)/shard_map/ppermute | solution.py:229
  29.8 0.1 fusion.3.back_ref
  29.9 1.6 %collective-permute-done = bf16[96,2560]{1,0:T(8,128)(2,1)S(1)} collective-permute-done((bf16[96,2560]{1,0:T(8,128)(2,1)}, bf16[96,2560]{1,0:T(8,128)(2,1)S(1)}, u32[]{:S(2)}, u32[]{:S(2)}) %collective-permute-start) | collective-permute-done | bytes 491552 | tf_op jit(solution)/shard_map/ppermute | solution.py:229
  31.5 0.2 maximum_select_fusion
  31.7 1.5 convolution_convert_fusion.1
  33.2 0.1 copy.21
  33.3 0.1 pad.9.clone
  33.5 60.2 %all-to-all-done.got_hbm = bf16[64,4,2688]{2,1,0:T(4,128)(2,1)S(1)} async-done(((bf16[64,4,2688]{2,1,0:T(4,128)(2,1)}), bf16[64,4,2688]{2,1,0:T(4,128)(2,1)S(1)}, u32[]{:S(2)}, u32[]{:S(2)}) %all-to-all-start) | async-done | bytes 1376288 | tf_op jit(solution)/shard_map/all_to_all | solution.py:225
  93.7 0.0 copy-start
  93.7 1.5 copy-done
  95.2 2.8 %slot_grads.1 = (bf16[32,192,128]{2,1,0:T(8,128)(2,1)S(1)}, bf16[2,112,128]{2,1,0:T(8,128)(2,1)S(1)}) custom-call(s32[1]{0:T(128)} %bitcast.core_ref, bf16[64,4,2688]{2,1,0:T(4,128)(2,1)S(1)} %all-to-all-done.got_hbm, bf16[2,128,3584]{2,1,0:T(8,128)(2,1)S(1)} %copy-done, bf16[256,128]{1,0:T(8,128)(2,1)S(1)} %bitcast.67, bf16[3,256,128]{2,1,0:T(8,128)(2,1)S(1)} %bitcast.66, ...), custom_call_target="tpu_custom_call" | custom-call | tf_op jit(solution)/shard_map/slot_grads/pallas_call | solution.py:168
  98.0 0.0 copy-start.1
  98.0 1.1 copy-done.1
  99.2 0.0 copy-start.4
  99.2 0.0 copy-start.6
  99.2 0.0 copy-start.2
  99.2 11.3 %all-to-all-start.1 = ((bf16[32,192,128]{2,1,0:T(8,128)(2,1)}), bf16[32,192,128]{2,1,0:T(8,128)(2,1)}, u32[]{:S(2)}, u32[]{:S(2)}) async-start(bf16[32,192,128]{2,1,0:T(8,128)(2,1)} %copy-done.1), calls=%async_computation.1 | async-start | bytes 3145728 | tf_op jit(solution)/shard_map/all_to_all | solution.py:253
  110.4 0.0 copy-start.5
  110.5 0.1 iota_add_fusion
  110.5 0.0 copy-done.4
  110.5 0.0 copy-done.6
  110.6 2.2 %collective-permute-start.1 = (bf16[112,128]{1,0:T(8,128)(2,1)S(1)}, bf16[112,128]{1,0:T(8,128)(2,1)S(1)}, u32[]{:S(2)}, u32[]{:S(2)}) collective-permute-start(bf16[112,128]{1,0:T(8,128)(2,1)S(1)} %dynamic-slice_bitcast_fusion.1), channel_id=1, source_target_pairs={{0,32},{32,0},{1,33},{33,1},{2,34},{34,2},{3,35},{35,3},{4,36},{36... | collective-permute-start | bytes 86024 | tf_op jit(solution)/shard_map/ppermute | solution.py:258
  112.8 0.8 collective-permute-done.1
  113.7 23.1 %all-gather = bf16[16,4,128]{2,1,0:T(4,128)(2,1)S(1)} all-gather(bf16[1,4,128]{2,1,0:T(4,128)(2,1)S(1)} %maximum_bitcast_fusion), channel_id=1, replica_groups=mesh['q'=16,'k'=2,'x'=2,'z'=16] {'z'}, dimensions={0}, use_global_device_ids=true | all-gather | bytes 17408 | tf_op jit(solution)/shard_map/all_gather | solution.py:264
  136.9 0.2 convolution_bitcast_fusion
  137.1 2.8 %collective-permute-start.2 = (f32[32,4]{0,1:T(4,128)S(1)}, f32[32,4]{0,1:T(4,128)S(1)}, u32[]{:S(2)}, u32[]{:S(2)}) collective-permute-start(f32[32,4]{0,1:T(4,128)S(1)} %get-tuple-element.19), channel_id=1, source_target_pairs={{0,16},{16,0},{1,17},{17,1},{2,18},{18,2},{3,19},{19,3},{4,20},{20... | collective-permute-start | bytes 1544 | tf_op jit(solution)/shard_map/ppermute | solution.py:272
  139.9 0.0 copy-done.2
  139.9 1.5 convolution_convert_fusion
  141.4 0.4 collective-permute-done.2
  141.8 0.1 copy.19
  141.9 0.1 reshape.144
  142.0 0.0 copy-done.5
  142.0 0.8 fusion
  142.8 6.9 %all-to-all-done.1 = bf16[32,192,128]{2,1,0:T(8,128)(2,1)} async-done(((bf16[32,192,128]{2,1,0:T(8,128)(2,1)}), bf16[32,192,128]{2,1,0:T(8,128)(2,1)}, u32[]{:S(2)}, u32[]{:S(2)}) %all-to-all-start.1) | async-done | bytes 1572896 | tf_op jit(solution)/shard_map/all_to_all | solution.py:253
  149.7 2.1 %add_parts.1 = (f32[2,80,128]{2,1,0:T(8,128)}, f32[2,112,128]{2,1,0:T(8,128)}) custom-call(bf16[16,2,192,128]{3,2,1,0:T(8,128)(2,1)} %bitcast.20.parts_ref), custom_call_target="tpu_custom_call" | custom-call | tf_op jit(solution)/shard_map/add_parts/pallas_call | solution.py:196
  (15 shorter events, 0.2 us)
Async XLA Ops:
  4.7 22.0 %copy-start.3 = (bf16[1,2,32,3,2560]{4,2,3,1,0:T(8,128)(2,1)S(1)}, bf16[1,2,32,3,2560]{4,2,3,1,0:T(8,128)(2,1)}, u32[]{:S(2)}) copy-start(bf16[1,2,32,3,2560]{4,2,3,1,0:T(8,128)(2,1)} %param.9) | copy-start | bytes 2949124
  4.7 89.0 %all-to-all-start = ((bf16[64,4,2688]{2,1,0:T(4,128)(2,1)}), bf16[64,4,2688]{2,1,0:T(4,128)(2,1)S(1)}, u32[]{:S(2)}, u32[]{:S(2)}) async-start(bf16[64,4,2688]{2,1,0:T(4,128)(2,1)} %get-tuple-element.10), calls=%async_computation | async-start | bytes 2752512 | tf_op jit(solution)/shard_map/all_to_all | solution.py:225
  27.6 4.0 %collective-permute-start = (bf16[96,2560]{1,0:T(8,128)(2,1)}, bf16[96,2560]{1,0:T(8,128)(2,1)S(1)}, u32[]{:S(2)}, u32[]{:S(2)}) collective-permute-start(bf16[96,2560]{1,0:T(8,128)(2,1)} %get-tuple-element.17), channel_id=1, source_target_pairs={{0,32},{32,0},{1,33},{33,1},{2,34},{34,2},{3,35},{35,3},{4,36},{36... | collective-permute-start | bytes 1474568 | tf_op jit(solution)/shard_map/ppermute | solution.py:229
  93.7 1.5 copy-start
  98.0 1.1 copy-start.1
  99.2 11.4 %copy-start.4 = (s32[128,1]{0,1:T(1,128)S(1)}, s32[128,1]{0,1:T(1,128)}, u32[]{:S(2)}) copy-start(s32[128,1]{0,1:T(1,128)} %param.8) | copy-start | bytes 1540
  99.2 11.4 %copy-start.6 = (s32[1,128]{1,0:T(1,128)S(1)}, s32[1,128]{1,0:T(1,128)}, u32[]{:S(2)}) copy-start(s32[1,128]{1,0:T(1,128)} %get-tuple-element.15) | copy-start | bytes 1540
  99.2 40.7 %copy-start.2 = (bf16[2,2560,128]{2,1,0:T(8,128)(2,1)S(1)}, bf16[2,2560,128]{2,1,0:T(8,128)(2,1)}, u32[]{:S(2)}) copy-start(bf16[2,2560,128]{2,1,0:T(8,128)(2,1)} %param.10) | copy-start | bytes 3932164
  99.2 50.5 %all-to-all-start.1 = ((bf16[32,192,128]{2,1,0:T(8,128)(2,1)}), bf16[32,192,128]{2,1,0:T(8,128)(2,1)}, u32[]{:S(2)}, u32[]{:S(2)}) async-start(bf16[32,192,128]{2,1,0:T(8,128)(2,1)} %copy-done.1), calls=%async_computation.1 | async-start | bytes 3145728 | tf_op jit(solution)/shard_map/all_to_all | solution.py:253
  110.4 31.6 %copy-start.5 = (bf16[128,1]{0,1:T(2,128)(2,1)S(1)}, bf16[128,1]{0,1:T(2,128)(2,1)}, u32[]{:S(2)}) copy-start(bf16[128,1]{0,1:T(2,128)(2,1)} %param.7) | copy-start | bytes 772
  110.6 3.1 %collective-permute-start.1 = (bf16[112,128]{1,0:T(8,128)(2,1)S(1)}, bf16[112,128]{1,0:T(8,128)(2,1)S(1)}, u32[]{:S(2)}, u32[]{:S(2)}) collective-permute-start(bf16[112,128]{1,0:T(8,128)(2,1)S(1)} %dynamic-slice_bitcast_fusion.1), channel_id=1, source_target_pairs={{0,32},{32,0},{1,33},{33,1},{2,34},{34,2},{3,35},{35,3},{4,36},{36... | collective-permute-start | bytes 86024 | tf_op jit(solution)/shard_map/ppermute | solution.py:258
  137.1 4.7 %collective-permute-start.2 = (f32[32,4]{0,1:T(4,128)S(1)}, f32[32,4]{0,1:T(4,128)S(1)}, u32[]{:S(2)}, u32[]{:S(2)}) collective-permute-start(f32[32,4]{0,1:T(4,128)S(1)} %get-tuple-element.19), channel_id=1, source_target_pairs={{0,16},{16,0},{1,17},{17,1},{2,18},{18,2},{3,19},{19,3},{4,20},{20... | collective-permute-start | bytes 1544 | tf_op jit(solution)/shard_map/ppermute | solution.py:272
